TPU v7x, 256 devices: a whole 4x4x8 slice. The times are simulated.
256 devices in a mesh: ctx: 64 (over z, x_lo, y), head: 4 (over x_hi, core).
Axes of the slice: x: 4 (x_hi: 2, x_lo: 2; x = x_hi * 2 + x_lo), y: 4, z: 8, core: 2. Of those that a mesh axis runs over, the one named last changes fastest.
Arguments:
- qkv: bfloat16 [3, 32768, 5120], P(None, 'ctx', 'head'), may hold values from -8 to 8
- step_size: float32 [32768, 8], P('ctx', 'head'), may hold values from 0.01 to 0.1
- fast_in: bfloat16 [8, 640, 1024], P('head'), may hold values from -1 to 1
- fast_out: bfloat16 [8, 512, 640], P('head'), may hold values from -1 to 1
Outputs:
- mixed: bfloat16 [32768, 5120], P('ctx', 'head')
All inputs are finite; a program needn't handle non-finite values.
Results may differ from a plain program's by a relative error of at most 0.0087.
Values may be sent and summed in bfloat16 or wider, within the bound.
A program may use at most 128 MiB of HBM per device.

v0:
```python
import jax
import jax.numpy as jnp
from jax import lax
from jax.sharding import PartitionSpec as P

ADIM = 128


EPS = 1e-06


def shifted(array, axis, by):
    size = lax.axis_size(axis)
    pairs = [(i, i + by) for i in range(size) if 0 <= i + by < size]
    return lax.ppermute(array, axis, pairs)


def silu_parts(gate_part):
    sigmoid_part = jax.nn.sigmoid(gate_part)
    return (gate_part * sigmoid_part, sigmoid_part * (1.0 + gate_part * (1.0 - sigmoid_part)))


def renorm(weight, update, norm_axis):
    old_value = weight.astype(jnp.float32)
    moved_value = old_value + update
    old_norm = jnp.sqrt(jnp.sum(old_value * old_value, axis=norm_axis, keepdims=True))
    new_norm = jnp.sqrt(jnp.sum(moved_value * moved_value, axis=norm_axis, keepdims=True))
    return (moved_value * (old_norm / (new_norm + EPS))).astype(jnp.bfloat16)


def local(qkv, step_size, fast_in, fast_out):
    tok_rows = qkv.shape[1]
    col_width = qkv.shape[2]
    per_device = fast_in.shape[0]
    head_width = fast_in.shape[1]
    hidden_dim = fast_out.shape[1]
    ctx_count = lax.axis_size("ctx")
    queries = qkv[0]
    key_rows = qkv[1]
    values = qkv[2]
    own_pair = qkv[1:]
    near_pair = shifted(own_pair, "ctx", 1)
    far_pair = shifted(own_pair, "ctx", 2)
    window_pair = jnp.concatenate([far_pair, near_pair, own_pair], axis=1)
    seq_start = lax.axis_index("ctx") * tok_rows
    row_pos = lax.broadcasted_iota(jnp.int32, (tok_rows, 3 * tok_rows), 0)
    col_pos = lax.broadcasted_iota(jnp.int32, (tok_rows, 3 * tok_rows), 1)
    allowed = (
        (col_pos > row_pos)
        & (col_pos <= row_pos + 2 * tok_rows)
        & (col_pos + seq_start >= 2 * tok_rows)
    )

    def one_head(head_index):
        offset = head_index * ADIM
        query_head = lax.dynamic_slice_in_dim(queries, offset, ADIM, 1)
        window_head = lax.dynamic_slice_in_dim(window_pair, offset, ADIM, 2)
        scores = jnp.dot(
            query_head, window_head[0].T, preferred_element_type=jnp.float32
        ) * ADIM ** (-0.5)
        scores = jnp.where(allowed, scores, -1e30)
        row_max = jnp.max(scores, axis=-1, keepdims=True)
        weights = jnp.where(allowed, jnp.exp(scores - row_max), 0.0)
        row_total = jnp.sum(weights, axis=-1, keepdims=True)
        probs_bf = (weights / row_total).astype(jnp.bfloat16)
        return jnp.dot(probs_bf, window_head[1], preferred_element_type=jnp.float32)

    head_count = col_width // ADIM
    attended = lax.map(one_head, jnp.arange(head_count, dtype=jnp.int32))
    attended = attended.transpose(1, 0, 2).reshape(tok_rows, col_width)
    query_three = queries.reshape(tok_rows, per_device, head_width)
    key_three = key_rows.reshape(tok_rows, per_device, head_width)
    value_three = values.reshape(tok_rows, per_device, head_width)
    projected = jnp.einsum("thd,hdf->thf", key_three, fast_in, preferred_element_type=jnp.float32)
    gate_part = projected[..., :hidden_dim]
    up_part = projected[..., hidden_dim:]
    activated, slope_part = silu_parts(gate_part)
    hidden = (activated * up_part).astype(jnp.bfloat16)
    scaled = (step_size[:, :, None] * value_three.astype(jnp.float32)).astype(jnp.bfloat16)
    back_part = jnp.einsum("thd,hfd->thf", scaled, fast_out, preferred_element_type=jnp.float32)
    pre_grad = jnp.concatenate(
        [back_part * up_part * slope_part, back_part * activated], axis=2
    ).astype(jnp.bfloat16)
    factor = (tok_rows * ctx_count) ** (-0.5)
    grad_in = jnp.einsum("thd,thf->hdf", key_three, pre_grad, preferred_element_type=jnp.float32)
    grad_out = jnp.einsum("thf,thd->hfd", hidden, scaled, preferred_element_type=jnp.float32)
    grad_in, grad_out = lax.psum((grad_in, grad_out), "ctx")
    new_in = renorm(fast_in, grad_in * factor, 1)
    new_out = renorm(fast_out, grad_out * factor, 1)
    query_proj = jnp.einsum("thd,hdf->thf", query_three, new_in, preferred_element_type=jnp.float32)
    query_act, unused_slope = silu_parts(query_proj[..., :hidden_dim])
    query_hidden = (query_act * query_proj[..., hidden_dim:]).astype(jnp.bfloat16)
    applied = jnp.einsum("thf,hfd->thd", query_hidden, new_out, preferred_element_type=jnp.float32)
    applied = applied.reshape(tok_rows, col_width)
    return (attended + applied).astype(jnp.bfloat16)


def solution(mesh):
    placed = (
        P(None, "ctx", "head"),
        P("ctx", "head"),
        P("head", None, None),
        P("head", None, None),
    )
    return jax.shard_map(
        local, mesh=mesh, in_specs=placed, out_specs=P("ctx", "head"), check_vma=False
    )
```

profile of v0, /device:TPU:2, one launch (start us, length us, event | category | flops | bytes accessed | tf_op | source)
XLA Modules:
  0.0 712.3 jit_solution(4803178432226219130)
XLA Ops:
  6.5 3.5 slice.31
  10.1 5.1 collective-permute-start
  20.7 4.3 reshape.39
  25.0 3.7 convolution_bitcast_fusion.1
  30.8 4.1 convolution_bitcast_fusion
  34.9 2.6 fusion.32
  39.2 2.6 copy.19
  44.4 33.5 %collective-permute-done = bf16[2,512,1280]{2,1,0:T(8,128)(2,1)} collective-permute-done((bf16[2,512,1280]{2,1,0:T(8,128)(2,1)}, bf16[2,512,1280]{2,1,0:T(8,128)(2,1)}, u32[]{:S(2)}, u32[]{:S(2)}) %collective-permute-start) | collective-permute-done | bytes 2621472 | tf_op jit(solution)/shard_map/ppermute | solution.py:15
  77.9 76.8 %collective-permute-done.1 = bf16[2,512,1280]{2,1,0:T(8,128)(2,1)} collective-permute-done((bf16[2,512,1280]{2,1,0:T(8,128)(2,1)}, bf16[2,512,1280]{2,1,0:T(8,128)(2,1)}, u32[]{:S(2)}, u32[]{:S(2)}) %collective-permute-start.1) | collective-permute-done | bytes 2621472 | tf_op jit(solution)/shard_map/ppermute | solution.py:15
  154.7 6.8 pad_maximum_fusion
  161.5 84.4 %while.11 = (s32[]{:T(128)}, f32[10,512,128]{1,2,0:T(8,128)}, s32[10]{0:T(128)S(1)}, bf16[512,1280]{0,1:T(8,128)(2,1)}, bf16[2,1536,1280]{2,1,0:T(8,128)(2,1)}, ...) while((s32[]{:T(128)}, f32[10,512,128]{1,2,0:T(8,128)}, ...), condition=%wide.region_3.4_spmd.clone, body=%wide.region_0.3_spmd.clone.sunk | while | flops 419953664 | bytes 10639555 | solution.py:69
  166.2 3.7 fusion.55
  174.6 3.7 fusion.55
  183.1 3.7 fusion.55
  191.5 3.7 fusion.55
  199.9 3.7 fusion.55
  208.4 3.7 fusion.55
  216.8 3.7 fusion.55
  225.3 3.7 fusion.55
  233.7 3.7 fusion.55
  242.2 3.8 fusion.55
  245.9 446.5 %all-reduce.3.cloned.1.call-done = (f32[2,512,640]{2,1,0:T(8,128)}, f32[2,640,1024]{1,2,0:T(8,128)}) async-done(((f32[2,512,640]{2,1,0:T(8,128)}, f32[2,640,1024]{1,2,0:T(8,128)}), (f32[2,512,640]{2,1,0:T(8,128)}, f32[2,640,1024]{1,2,0:T(8,128)})) %all-reduce.3.cloned.1.call-update) | async-done | bytes 7864336 | tf_op jit(solution)/shard_map/psum | solution.py:87
  692.4 2.8 fusion.14
  695.2 3.9 fusion.13
  (69 shorter events, 58.7 us)
Async XLA Ops:
  6.5 685.9 %all-reduce.3.cloned.1.call-start = ((), (), s32[]{:S(2)}) async-start(), calls=%async_computation | async-start | bytes 15728640 | tf_op jit(solution)/shard_map/psum | solution.py:87
  6.5 11.2 %copy-start.2 = (bf16[3,512,1280]{2,1,0:T(8,128)(2,1)S(1)}, bf16[3,512,1280]{2,1,0:T(8,128)(2,1)}, u32[]{:S(2)}) copy-start(bf16[3,512,1280]{2,1,0:T(8,128)(2,1)} %param.6) | copy-start | bytes 11796484
  10.1 67.9 %collective-permute-start = (bf16[2,512,1280]{2,1,0:T(8,128)(2,1)}, bf16[2,512,1280]{2,1,0:T(8,128)(2,1)}, u32[]{:S(2)}, u32[]{:S(2)}) collective-permute-start(bf16[2,512,1280]{2,1,0:T(8,128)(2,1)} %slice.31), channel_id=1, source_target_pairs={{0,8},{4,12},{8,16},{12,20},{16,24},{20,28},{24,32},{28,36},{32,40... | collective-permute-start | bytes 7864328 | tf_op jit(solution)/shard_map/ppermute | solution.py:15
  15.2 139.6 %collective-permute-start.1 = (bf16[2,512,1280]{2,1,0:T(8,128)(2,1)}, bf16[2,512,1280]{2,1,0:T(8,128)(2,1)}, u32[]{:S(2)}, u32[]{:S(2)}) collective-permute-start(bf16[2,512,1280]{2,1,0:T(8,128)(2,1)} %slice.31), channel_id=1, source_target_pairs={{0,4},{4,8},{8,12},{12,16},{16,20},{20,24},{24,28},{28,32},{32,36}... | collective-permute-start | bytes 7864328 | tf_op jit(solution)/shard_map/ppermute | solution.py:15
  25.0 3.7 copy-start.7
  25.0 3.7 copy-start.8
  25.0 3.8 copy-start.10
  37.5 1.7 copy-start.3
  245.9 449.2 %copy-start = (bf16[2,640,1024]{1,2,0:T(8,128)(2,1)S(1)}, bf16[2,640,1024]{1,2,0:T(8,128)(2,1)}, u32[]{:S(2)}) copy-start(bf16[2,640,1024]{1,2,0:T(8,128)(2,1)} %copy.19) | copy-start | bytes 7864324
  695.2 4.0 copy-start.1
  695.2 4.4 copy-start.4
  699.6 2.0 copy-start.6
  699.6 2.1 copy-start.9
  701.7 1.7 copy-start.5
Sparse Core Ops, SparseCore 0:
  37.7 654.7 all-reduce.2
where the time goes:
time: 716 us; the launch traced here: 712 us
  waiting for transfers between devices  557 us (78%)
  matrix products  76 us (11%)
  other arithmetic  28 us (4%)
  local copies, waits for them, and re-layouts  23.8 us (3%)
  between operations  13.5 us (2%)
  starting transfers between devices  7.68 us (1%)
    psum x1, waiting for transfers between devices, local(): grad_in, grad_out = lax.psum((grad_in, grad_out), 'ctx')  446 us
    ppermute x2, waiting for transfers between devices, shifted(): return lax.ppermute(array, axis, pairs)  110 us
    dot_general x10, matrix products, one_head(): return jnp.dot(probs_bf, window_head[1], preferred_element_type=jnp.float32)  37.4 us
    dot_general x10, matrix products, one_head(): jnp.dot(query_head, window_head[0].T, preferred_element_type=jnp.float32)  23.1 us
  transfers between devices with their start and end apart: 3, of which 3 were waited for; matrix products, arithmetic and copies ran while one was open for 15% of the time, Pallas kernels for 0%

commit v1 on v0

v1 whole, which is shorter than its diff:
```python
import functools

import jax
import jax.numpy as jnp
from jax import lax
from jax.experimental import pallas as pl
from jax.experimental.pallas import tpu as pltpu
from jax.sharding import PartitionSpec as P

ADIM = 128
FH = 512
HD = 640
TOK = 512
COLS = 1280
EPS = 1e-06
FACTOR = 32768.0 ** -0.5
SCALE = 1.4426950408889634 * ADIM ** -0.5
STRAND = 256
PLUS = (0, 1, 2)
MINUS = (3, 4)
BF = jnp.bfloat16
F32 = jnp.float32
MESH = pl.DeviceIdType.MESH
MESSAGES = 160


def nt(a, b):
    return lax.dot_general(a, b, (((1,), (1,)), ((), ())), preferred_element_type=F32)


def nn(a, b):
    return jnp.dot(a, b, preferred_element_type=F32)


def mult(index, of):
    return pl.multiple_of(index, of)


def kernel(
    qkv, step, w_in, w_out, out,
    kv, q, wi, wo, g, mi, mo, r1, r0, xb, x1, t1, u0, u1, ys, yr, pst, sst, att,
    local_sem, ss, rs,
):
    c = lax.axis_index("ctx")
    head = lax.axis_index("head")
    y = lax.rem(c, 4)
    x = lax.rem(c // 4, 2)
    z = c // 8
    other = 1 - x
    s_own = 2 * z + x

    def at(zz, xx, yy):
        return (8 * lax.rem(zz + 16, 8) + 4 * xx + lax.rem(yy + 8, 4), head)

    y_dev = {j: at(z, x, y + j) for j in (-1, 1, 2, 3)}
    z_dev = (at(z + 1, x, y), at(z - 1, x, y))
    x_dev = at(z, other, y)
    next_dev = (lax.rem(c + 4, 64), head)
    prev_dev = (lax.rem(c + 60, 64), head)

    used = [0]
    sent = []

    def message(size_ref, always=True):
        index = used[0]
        used[0] += 1
        if always:
            sent.append((index, size_ref))
        return index

    def copy(index, src, dst, device):
        return pltpu.make_async_remote_copy(
            src_ref=src, dst_ref=dst, send_sem=ss.at[index], recv_sem=rs.at[index],
            device_id=device, device_id_type=MESH,
        )

    def landed(index, ref):
        copy(index, ref, ref, x_dev).wait_recv()

    barrier = pltpu.get_barrier_semaphore()
    for device in (y_dev[1], y_dev[2], y_dev[3], *z_dev, x_dev, next_dev, prev_dev):
        pl.semaphore_signal(barrier, inc=1, device_id=device, device_id_type=MESH)

    locals_ = []

    def fetch(src, dst):
        cp = pltpu.make_async_copy(src, dst, local_sem.at[len(locals_)])
        cp.start()
        locals_.append(cp)

    own_rows = pl.ds(2 * TOK, TOK)
    near_rows = pl.ds(TOK, TOK)
    far_rows = pl.ds(0, TOK)
    fetch(qkv.at[pl.ds(1, 2)], kv.at[:, own_rows])
    fetch(w_in, wi)
    fetch(w_out, wo)
    fetch(qkv.at[0], q)
    pl.semaphore_wait(barrier, 8)

    def cols(strand):
        return pl.ds(strand * STRAND, STRAND)

    def own(strand):
        return qkv.at[pl.ds(1, 2), :, cols(strand)]

    def near(strand):
        return kv.at[:, near_rows, cols(strand)]

    def far(strand):
        return kv.at[:, far_rows, cols(strand)]

    pid = {}
    for strand in PLUS:
        for name in ("near", "far", "c3", "c2"):
            pid[strand, name] = message(None, False)
    for strand in MINUS:
        for name in ("u1", "u2", "u3", "cfar", "cnear"):
            pid[strand, name] = message(None, False)

    def plus_start(strand):
        @pl.when(y < 3)
        def _():
            copy(pid[strand, "near"], own(strand), near(strand), y_dev[1]).start()

        @pl.when(y == 3)
        def _():
            copy(pid[strand, "c3"], own(strand), pst.at[strand, 0], next_dev).start()

    def plus_cross_near(strand):
        @pl.when(y == 3)
        def _():
            landed(pid[strand, "c3"], pst.at[strand, 0])
            copy(pid[strand, "near"], pst.at[strand, 0], near(strand), y_dev[1]).start()

    def plus_forward(strand):
        landed(pid[strand, "near"], near(strand))

        @pl.when(y < 3)
        def _():
            copy(pid[strand, "far"], near(strand), far(strand), y_dev[1]).start()

        @pl.when(y == 3)
        def _():
            copy(pid[strand, "c2"], near(strand), pst.at[strand, 1], next_dev).start()

    def plus_cross_far(strand):
        @pl.when(y == 3)
        def _():
            landed(pid[strand, "c2"], pst.at[strand, 1])
            copy(pid[strand, "far"], pst.at[strand, 1], far(strand), y_dev[1]).start()

    def plus_done(strand):
        landed(pid[strand, "far"], far(strand))

    def minus_start(strand):
        m = strand - MINUS[0]
        copy(pid[strand, "u1"], own(strand), sst.at[m, 0], y_dev[-1]).start()

    def minus_second(strand):
        m = strand - MINUS[0]
        landed(pid[strand, "u1"], sst.at[m, 0])

        @pl.when(y == 3)
        def _():
            copy(pid[strand, "u2"], sst.at[m, 0], far(strand), y_dev[-1]).start()

        @pl.when(y == 0)
        def _():
            copy(pid[strand, "u2"], sst.at[m, 0], far(strand), y_dev[-1]).start()

        @pl.when((y == 1) | (y == 2))
        def _():
            copy(pid[strand, "u2"], sst.at[m, 0], sst.at[m, 1], y_dev[-1]).start()

    def minus_third(strand):
        m = strand - MINUS[0]

        @pl.when(y >= 2)
        def _():
            landed(pid[strand, "u2"], far(strand))
            copy(pid[strand, "u3"], far(strand), near(strand), y_dev[-1]).start()

        @pl.when(y == 1)
        def _():
            landed(pid[strand, "u2"], sst.at[m, 1])
            copy(pid[strand, "u3"], sst.at[m, 1], sst.at[m, 2], y_dev[-1]).start()
            copy(pid[strand, "cfar"], sst.at[m, 1], far(strand), next_dev).start()

        @pl.when(y == 0)
        def _():
            landed(pid[strand, "u2"], sst.at[m, 1])
            copy(pid[strand, "u3"], sst.at[m, 1], near(strand), y_dev[-1]).start()
            copy(pid[strand, "cfar"], sst.at[m, 1], far(strand), next_dev).start()

    def minus_cross(strand):
        m = strand - MINUS[0]

        @pl.when(y == 0)
        def _():
            landed(pid[strand, "u3"], sst.at[m, 2])
            copy(pid[strand, "cnear"], sst.at[m, 2], near(strand), next_dev).start()

    def minus_done(strand):
        @pl.when(y > 0)
        def _():
            landed(pid[strand, "u3"], near(strand))

        @pl.when(y == 0)
        def _():
            landed(pid[strand, "cnear"], near(strand))

        @pl.when(y <= 1)
        def _():
            landed(pid[strand, "cfar"], far(strand))

    def halo_sends_done():
        for strand in PLUS:
            piece = near(strand)
            copy(pid[strand, "near"], piece, piece, x_dev).wait_send()
            copy(pid[strand, "far"], piece, piece, x_dev).wait_send()

            @pl.when(y == 3)
            def _():
                copy(pid[strand, "c3"], piece, piece, x_dev).wait_send()
                copy(pid[strand, "c2"], piece, piece, x_dev).wait_send()

        for strand in MINUS:
            piece = near(strand)
            for name in ("u1", "u2", "u3"):
                copy(pid[strand, name], piece, piece, x_dev).wait_send()

            @pl.when(y <= 1)
            def _():
                copy(pid[strand, "cfar"], piece, piece, x_dev).wait_send()

            @pl.when(y == 0)
            def _():
                copy(pid[strand, "cnear"], piece, piece, x_dev).wait_send()

    def gradients(h):
        hc = pl.ds(h * HD, HD)
        keys = kv[0, own_rows, hc]
        vals = kv[1, own_rows, hc]
        rate = step[:, h:h + 1]
        scaled = (rate * vals.astype(F32)).astype(BF)
        gate = nt(wi[h, 0:FH], keys)
        up = nt(wi[h, FH:2 * FH], keys)
        back = nt(wo[h], scaled)
        sig = jax.nn.sigmoid(gate)
        act = gate * sig
        hidden = (act * up).astype(BF)
        d_gate = (back * up * sig * (1.0 + gate * (1.0 - sig))).astype(BF)
        d_up = (back * act).astype(BF)
        g_gate = nn(d_gate, keys).astype(BF)
        for s in range(8):
            g[h, s, 0:64] = g_gate[64 * s:64 * s + 64]
        g_up = nn(d_up, keys).astype(BF)
        for s in range(8):
            g[h, 8 + s, 0:64] = g_up[64 * s:64 * s + 64]
        g_out = nn(hidden, scaled).astype(BF)
        for s in range(16):
            g[h, s, 64:96] = g_out[32 * s:32 * s + 32]

    def add(dst, src):
        dst[...] = (dst[...].astype(F32) + src[...].astype(F32)).astype(BF)

    def z_of(direction, distance):
        offset = distance if direction == 0 else -distance
        return lax.rem(z + offset + 8, 8)

    def chains(k):
        for direction in (0, 1):
            for half in (direction, 1 - direction):
                start = 0 if half == direction else 1
                if k >= start:
                    yield direction, half, k == start

    ring1 = {(d, h, k): message(r1.at[0, 0, 0]) for k in range(4) for d, h, _ in chains(k)}
    ring0 = {(d, h, k): message(r0.at[0, 0, 0]) for k in range(4) for d, h, _ in chains(k)}
    cross0 = [message(xb.at[0]) for _ in range(8)]
    cross1 = message(x1)

    def ring1_step(k):
        for direction, half, first in chains(k):
            part = g.at[1, 2 * z_of(direction, 4 - k) + half]
            if first:
                src = part
            else:
                src = r1.at[direction, half, k - 1]
                landed(ring1[direction, half, k - 1], src)
                add(src, part)
            copy(ring1[direction, half, k], src, r1.at[direction, half, k], z_dev[direction]).start()

    def ring1_end():
        for direction in (0, 1):
            for half in (0, 1):
                landed(ring1[direction, half, 3], r1.at[direction, half, 3])

        def total(half):
            return (
                g[1, 2 * z + half].astype(F32)
                + r1[0, half, 3].astype(F32)
                + r1[1, half, 3].astype(F32)
            )

        t1[...] = total(other).astype(BF)
        copy(cross1, t1, x1, x_dev).start()
        u1[...] = total(x)

    slots = [(0, 4), (0, 3), (1, 3), (0, 2), (1, 2), (0, 1), (1, 1), (0, 0)]
    slot_of = {pair: i for i, pair in enumerate(slots)}
    slot_of[1, 4] = 0

    def cross0_start():
        for i, (direction, distance) in enumerate(slots):
            copy(
                cross0[i], g.at[0, 2 * z_of(direction, distance) + other], xb.at[i], x_dev
            ).start()

    def cross0_add(i):
        landed(cross0[i], xb.at[i])
        direction, distance = slots[i]
        add(xb.at[i], g.at[0, 2 * z_of(direction, distance) + x])

    def ring0_step(k):
        for i in {0: (0,), 1: (1, 2), 2: (3, 4), 3: (5, 6)}[k]:
            cross0_add(i)
        for direction, half, first in chains(k):
            part = xb.at[slot_of[direction, 4 - k], pl.ds(48 * half, 48)]
            if first:
                src = part
            else:
                src = r0.at[direction, half, k - 1]
                landed(ring0[direction, half, k - 1], src)
                add(src, part)
            copy(ring0[direction, half, k], src, r0.at[direction, half, k], z_dev[direction]).start()

    def ring0_end():
        cross0_add(7)
        for half in (0, 1):
            rows = pl.ds(48 * half, 48)
            for direction in (0, 1):
                landed(ring0[direction, half, 3], r0.at[direction, half, 3])
            u0[rows] = (
                xb[7, rows].astype(F32) + r0[0, half, 3].astype(F32) + r0[1, half, 3].astype(F32)
            )

    y_sum = {j: message(ys.at[0]) for j in (1, 2, 3)}

    def y_reduce():
        landed(cross1, x1)
        u1[...] = u1[...] + x1[...].astype(F32)
        for p in range(4):
            ys[p, 0:16] = u0[16 * p:16 * p + 16].astype(BF)
            ys[p, 16:32] = u1[16 * p:16 * p + 16].astype(BF)
            source = u0 if p < 2 else u1
            first = 64 + 16 * (p % 2)
            ys[p, 32:48] = source[first:first + 16].astype(BF)
        for j in (1, 2, 3):
            copy(y_sum[j], ys.at[lax.rem(y + j, 4)], yr.at[j - 1], y_dev[j]).start()
        for j in (1, 2, 3):
            landed(y_sum[j], yr.at[j - 1])

    in_row = mult(64 * s_own + 16 * y, 16)
    out_head = y // 2
    out_row = mult(32 * s_own + 16 * lax.rem(y, 2), 16)

    def renorm():
        total = ys[y].astype(F32)
        for j in range(3):
            total = total + yr[j].astype(F32)
        for h in (0, 1):
            old = wi[h, pl.ds(in_row, 16)].astype(F32)
            moved = old + total[16 * h:16 * h + 16] * FACTOR
            old_norm = jnp.sqrt(jnp.sum(old * old, axis=1, keepdims=True))
            new_norm = jnp.sqrt(jnp.sum(moved * moved, axis=1, keepdims=True))
            mi[h, pl.ds(in_row, 16)] = (moved * (old_norm / (new_norm + EPS))).astype(BF)
        old = wo[out_head, pl.ds(out_row, 16)].astype(F32)
        mo[out_head, pl.ds(out_row, 16)] = (old + total[32:48] * FACTOR).astype(BF)

    sixteen = mi.at[0, pl.ds(0, 16)]
    y_all = {(j, i): message(sixteen) for j in (1, 2, 3) for i in range(3)}

    def y_gather():
        pieces = (
            mi.at[0, pl.ds(in_row, 16)],
            mi.at[1, pl.ds(in_row, 16)],
            mo.at[out_head, pl.ds(out_row, 16)],
        )
        for j in (1, 2, 3):
            for i, piece in enumerate(pieces):
                copy(y_all[j, i], piece, piece, y_dev[j]).start()
        for j in (1, 2, 3):
            yy = lax.rem(y - j + 4, 4)
            row = mult(64 * s_own + 16 * yy, 16)
            landed(y_all[j, 0], mi.at[0, pl.ds(row, 16)])
            landed(y_all[j, 1], mi.at[1, pl.ds(row, 16)])
            row = mult(32 * s_own + 16 * lax.rem(yy, 2), 16)
            landed(y_all[j, 2], mo.at[yy // 2, pl.ds(row, 16)])

    def chunk(h, zz, part=None, xx=None):
        rows = 128 if h == 1 else 64
        first = 128 * zz + (64 * (x if xx is None else xx) if h == 0 or xx is not None else 0)
        if xx is not None:
            rows = 64
        n_in, f_in = rows, first
        n_out, f_out = rows // 2, first // 2
        if part is not None:
            n_in, n_out = n_in // 2, n_out // 2
            f_in = f_in + part * n_in
            f_out = f_out + part * n_out
        return (
            mi.at[h, pl.ds(mult(f_in, 16), n_in)],
            mo.at[h, pl.ds(mult(f_out, 16), n_out)],
        )

    def pair_ids(h, part=None, xx=None):
        return tuple(message(ref) for ref in chunk(h, 0, part, xx))

    def push(ids, refs, device):
        for index, ref in zip(ids, refs):
            copy(index, ref, ref, device).start()

    def pushed(ids, refs):
        for index, ref in zip(ids, refs):
            landed(index, ref)

    gather = {
        (h, j, d): pair_ids(h, d if j == 4 else None)
        for h in (0, 1) for j in (1, 2, 3, 4) for d in (0, 1)
    }
    share0 = [pair_ids(0) for _ in range(8)]
    share1 = pair_ids(1, None, x)

    def gather_send(h, j):
        for d in (0, 1):
            part = d if j == 4 else None
            push(gather[h, j, d], chunk(h, z_of(1 - d, j - 1), part), z_dev[d])

    def gather_wait(h, j):
        for d in (0, 1):
            part = d if j == 4 else None
            pushed(gather[h, j, d], chunk(h, z_of(1 - d, j), part))

    share_order = [(0, 0)] + [(d, j) for j in (1, 2, 3) for d in (0, 1)] + [(0, 4)]

    def share_send(j):
        for i, (d, jj) in enumerate(share_order):
            if jj == j:
                push(share0[i], chunk(0, z_of(1 - d, j)), x_dev)

    def share_wait():
        for i, (d, j) in enumerate(share_order):
            pushed(share0[i], chunk(0, z_of(1 - d, j), None, other))

    row = lax.broadcasted_iota(jnp.int32, (256, 256), 0)
    col = lax.broadcasted_iota(jnp.int32, (256, 256), 1)
    far_off = jnp.where(c < 2, 1e30, 0.0).astype(F32)
    near_off = jnp.where(c < 1, 1e30, 0.0).astype(F32)

    def attention(a, rb):
        ac = pl.ds(a * ADIM, ADIM)
        window = pl.ds(rb * 256, 1280)
        scores = nt(q[pl.ds(rb * 256, 256), ac], kv[0, window, ac])
        offs = (far_off, far_off, near_off, near_off, None, None)[rb:rb + 5]
        blocks = [scores[:, 256 * b:256 * b + 256] for b in range(5)]
        blocks[0] = jnp.where(col > row, blocks[0], -1e30)
        blocks[4] = jnp.where(col <= row, blocks[4], -1e30)
        top = None
        for block, off in zip(blocks, offs):
            peak = jnp.max(block, axis=1, keepdims=True)
            if off is not None:
                peak = peak - off
            top = peak if top is None else jnp.maximum(top, peak)
        base = top * SCALE
        weights = []
        for block, off in zip(blocks, offs):
            weights.append(jnp.exp2(block * SCALE - (base if off is None else base + off)))
        total = sum(jnp.sum(w, axis=1, keepdims=True) for w in weights)
        probs = jnp.concatenate([w.astype(BF) for w in weights], axis=1)
        mixed = nn(probs, kv[1, window, ac])
        att[pl.ds(rb * 256, 256), ac] = mixed / total

    def attend(strand):
        for a in (2 * strand, 2 * strand + 1):
            for rb in (0, 1):
                attention(a, rb)

    def apply(h):
        hc = pl.ds(h * HD, HD)
        queries = q[:, hc]
        gate = nt(queries, mi[h, 0:FH])
        up = nt(queries, mi[h, FH:2 * FH])
        hidden = (gate * jax.nn.sigmoid(gate) * up).astype(BF)
        old = wo[h].astype(F32)
        new = mo[h].astype(F32)
        old_norm = jnp.sqrt(jnp.sum(old * old, axis=0, keepdims=True))
        new_norm = jnp.sqrt(jnp.sum(new * new, axis=0, keepdims=True))
        applied = nn(hidden, mo[h]) * (old_norm / (new_norm + EPS))
        out[:, hc] = (att[:, hc] + applied).astype(BF)

    plus_start(0)
    minus_start(3)
    locals_[0].wait()
    locals_[1].wait()
    locals_[2].wait()
    gradients(0)
    cross0_start()
    plus_start(1)
    minus_start(4)
    gradients(1)
    ring1_step(0)
    plus_start(2)
    ring1_step(1)
    plus_cross_near(0)
    plus_forward(0)
    ring1_step(2)
    minus_second(3)
    ring1_step(3)
    ring0_step(0)
    ring1_end()
    plus_cross_near(1)
    plus_forward(1)
    minus_second(4)
    ring0_step(1)
    plus_cross_far(0)
    plus_cross_near(2)
    ring0_step(2)
    minus_third(3)
    plus_forward(2)
    ring0_step(3)
    ring0_end()
    y_reduce()
    renorm()
    y_gather()
    gather_send(0, 1)
    push(share1, chunk(1, z, None, x), x_dev)
    share_send(0)
    plus_cross_far(1)
    minus_third(4)
    pushed(share1, chunk(1, z, None, other))
    gather_send(1, 1)
    locals_[3].wait()
    plus_done(0)
    for j in (1, 2, 3):
        gather_wait(0, j)
        gather_send(0, j + 1)
        share_send(j)
        if j == 1:
            plus_cross_far(2)
            minus_cross(3)
        if j == 2:
            minus_cross(4)
        gather_wait(1, j)
        gather_send(1, j + 1)
    gather_wait(0, 4)
    share_send(4)
    attend(0)
    plus_done(1)
    attend(1)
    plus_done(2)
    attend(2)
    minus_done(3)
    attend(3)
    minus_done(4)
    attend(4)
    gather_wait(1, 4)
    apply(1)
    share_wait()
    apply(0)
    halo_sends_done()
    for index, ref in sent:
        copy(index, ref, ref, x_dev).wait_send()


def local(qkv, step_size, fast_in, fast_out):
    anywhere = pl.BlockSpec(memory_space=pl.ANY)
    vmem = pl.BlockSpec(memory_space=pltpu.VMEM)
    return pl.pallas_call(
        kernel,
        out_shape=jax.ShapeDtypeStruct((TOK, COLS), BF),
        in_specs=[anywhere, vmem, anywhere, anywhere],
        out_specs=vmem,
        scratch_shapes=[
            pltpu.VMEM((2, 3 * TOK, COLS), BF),
            pltpu.VMEM((TOK, COLS), BF),
            pltpu.VMEM((2, 2 * FH, HD), BF),
            pltpu.VMEM((2, FH, HD), BF),
            pltpu.VMEM((2, 16, 96, HD), BF),
            pltpu.VMEM((2, 2 * FH, HD), BF),
            pltpu.VMEM((2, FH, HD), BF),
            pltpu.VMEM((2, 2, 4, 96, HD), BF),
            pltpu.VMEM((2, 2, 4, 48, HD), BF),
            pltpu.VMEM((8, 96, HD), BF),
            pltpu.VMEM((96, HD), BF),
            pltpu.VMEM((96, HD), BF),
            pltpu.VMEM((96, HD), F32),
            pltpu.VMEM((96, HD), F32),
            pltpu.VMEM((4, 48, HD), BF),
            pltpu.VMEM((3, 48, HD), BF),
            pltpu.VMEM((3, 2, 2, TOK, STRAND), BF),
            pltpu.VMEM((2, 3, 2, TOK, STRAND), BF),
            pltpu.VMEM((TOK, COLS), F32),
            pltpu.SemaphoreType.DMA((4,)),
            pltpu.SemaphoreType.DMA((MESSAGES,)),
            pltpu.SemaphoreType.DMA((MESSAGES,)),
        ],
        name="ttt_layer",
        compiler_params=pltpu.CompilerParams(
            collective_id=0, has_side_effects=True, vmem_limit_bytes=62 * 2**20
        ),
    )(qkv, step_size, fast_in.transpose(0, 2, 1), fast_out)


def solution(mesh):
    placed = (
        P(None, "ctx", "head"),
        P("ctx", "head"),
        P("head", None, None),
        P("head", None, None),
    )
    return jax.shard_map(
        local, mesh=mesh, in_specs=placed, out_specs=P("ctx", "head"), check_vma=False
    )
```

time: 716 us -> 213 us (0.30)
  waiting for transfers between devices: 557 us -> 0 us
  Pallas kernels: 0 us -> 205 us
  matrix products: 76 us -> 0 us
  other arithmetic: 28 us -> 0 us
  local copies, waits for them, and re-layouts: 23.8 us -> 8.38 us
  between operations: 13.5 us -> 0.01 us
  starting transfers between devices: 7.68 us -> 0 us
    psum x1 -> x0, waiting for transfers between devices: 446 us -> none  [local(): grad_in, grad_out = lax.psum((grad_in, grad_out), 'ctx')]
    pallas_call x0 -> x1, Pallas kernels: none -> 205 us  [local(): pl.pallas_call(kernel, out_shape=jax.ShapeDtypeStruct((TOK, COLS), BF), i...]
    ppermute x2 -> x0, waiting for transfers between devices: 110 us -> none  [shifted(): return lax.ppermute(array, axis, pairs)]
    dot_general x26 -> x0, matrix products: 76 us -> none  [the longest x10 37.4 us: one_head(): return jnp.dot(probs_bf, window_head[1], preferred_element_type=jnp.float32)]
    reduce_sum x12 -> x0, other arithmetic: 18.4 us -> none  [the longest x10 11.7 us: one_head(): row_total = jnp.sum(weights, axis=-1, keepdims=True)]
    ppermute x2 -> x0, starting transfers between devices: 7.68 us -> none  [shifted(): return lax.ppermute(array, axis, pairs)]
  transfers between devices with their start and end apart: 3 -> 0, of which waited for: 3 -> 0; matrix products, arithmetic and copies ran while one was open for 15% -> 0% of each run, Pallas kernels for 0% -> 0%
where the time goes in v1:
time: 213 us
  Pallas kernels  205 us (96%)
  local copies, waits for them, and re-layouts  8.38 us (4%)
    pallas_call x1, Pallas kernels, local(): pl.pallas_call(kernel, out_shape=jax.ShapeDtypeStruct((TOK, COLS), BF), i...  205 us
    unnamed x3, local copies, waits for them, and re-layouts  8.38 us

profile of v1, /device:TPU:2, one launch (start us, length us, event | category | flops | bytes accessed | tf_op | source)
XLA Modules:
  0.0 213.2 jit_solution(157170756042411373)
XLA Ops:
  0.0 1.5 copy.6.step
  1.5 4.4 %copy.5 = bf16[2,640,1024]{1,2,0:T(8,128)(2,1)} copy(bf16[2,640,1024]{2,1,0:T(8,128)(2,1)} %param.6) | data formatting | bytes 5242880 | tf_op args[2]
  5.9 204.8 %ttt_layer.1 = bf16[512,1280]{1,0:T(8,128)(2,1)} custom-call(bf16[3,512,1280]{2,1,0:T(8,128)(2,1)} %qkv.1, f32[512,2]{1,0:T(8,128)} %copy.6.step, bf16[2,1024,640]{2,1,0:T(8,128)(2,1)} %bitcast.1, bf16[2,512,640]{2,1,0:T(8,128)(2,1)} %w_out.1), custom_call_target="tpu_custom_call" | custom-call | tf_op jit(solution)/shard_map/ttt_layer/pallas_call | solution.py:579
  210.7 2.5 %copy.8 = bf16[512,1280]{1,0:T(8,128)(2,1)} copy(bf16[512,1280]{1,0:T(8,128)(2,1)} %ttt_layer.1) | data formatting | bytes 2621440

commit v2 on v1

--- a/solution.py
+++ b/solution.py
@@ -18,6 +18,8 @@
 STRAND = 256
 PLUS = (0, 1, 2)
 MINUS = (3, 4)
+CROSS_NEAR_FIRST = {0: True, 1: False, 2: True}
+CROSS_FAR_FIRST = {0: False, 1: True, 2: True}
 BF = jnp.bfloat16
 F32 = jnp.float32
 MESH = pl.DeviceIdType.MESH
@@ -111,66 +113,97 @@
 
     pid = {}
     for strand in PLUS:
-        for name in ("near", "far", "c3", "c2"):
+        for name in ("near", "far", "c3", "c2", "xnear", "xfar"):
             pid[strand, name] = message(None, False)
     for strand in MINUS:
-        for name in ("u1", "u2", "u3", "cfar", "cnear"):
+        for name in ("u1", "u2", "u3", "cfar"):
             pid[strand, name] = message(None, False)
 
-    def plus_start(strand):
-        @pl.when(y < 3)
-        def _():
-            copy(pid[strand, "near"], own(strand), near(strand), y_dev[1]).start()
-
-        @pl.when(y == 3)
-        def _():
-            copy(pid[strand, "c3"], own(strand), pst.at[strand, 0], next_dev).start()
-
-    def plus_cross_near(strand):
-        @pl.when(y == 3)
-        def _():
-            landed(pid[strand, "c3"], pst.at[strand, 0])
-            copy(pid[strand, "near"], pst.at[strand, 0], near(strand), y_dev[1]).start()
-
-    def plus_forward(strand):
-        landed(pid[strand, "near"], near(strand))
-
-        @pl.when(y < 3)
-        def _():
-            copy(pid[strand, "far"], near(strand), far(strand), y_dev[1]).start()
-
-        @pl.when(y == 3)
-        def _():
-            copy(pid[strand, "c2"], near(strand), pst.at[strand, 1], next_dev).start()
-
-    def plus_cross_far(strand):
-        @pl.when(y == 3)
-        def _():
-            landed(pid[strand, "c2"], pst.at[strand, 1])
-            copy(pid[strand, "far"], pst.at[strand, 1], far(strand), y_dev[1]).start()
+    def halo(strand, name, src, dst, device):
+        copy(pid[strand, name], src, dst, device).start()
+
+    def plus_start(strand, last=True, rest=True):
+        if rest:
+            @pl.when(y < 3)
+            def _():
+                halo(strand, "near", own(strand), near(strand), y_dev[1])
+
+        if last:
+            @pl.when(y == 3)
+            def _():
+                halo(strand, "c3", own(strand), pst.at[strand, 0],
+                     next_dev if CROSS_NEAR_FIRST[strand] else y_dev[1])
+
+    def plus_relay_near(strand):
+        if CROSS_NEAR_FIRST[strand]:
+            @pl.when(y == 3)
+            def _():
+                landed(pid[strand, "c3"], pst.at[strand, 0])
+                halo(strand, "near", pst.at[strand, 0], near(strand), y_dev[1])
+        else:
+            @pl.when(y == 0)
+            def _():
+                landed(pid[strand, "c3"], pst.at[strand, 0])
+                halo(strand, "xnear", pst.at[strand, 0], near(strand), next_dev)
+
+    def plus_relay_far(strand):
+        if CROSS_FAR_FIRST[strand]:
+            @pl.when(y == 3)
+            def _():
+                landed(pid[strand, "c2"], pst.at[strand, 1])
+                halo(strand, "far", pst.at[strand, 1], far(strand), y_dev[1])
+        else:
+            @pl.when(y == 0)
+            def _():
+                landed(pid[strand, "c2"], pst.at[strand, 1])
+                halo(strand, "xfar", pst.at[strand, 1], far(strand), next_dev)
+
+    def plus_forward(strand, ys_=(0, 1, 2, 3)):
+        for yy in ys_:
+            @pl.when(y == yy)
+            def _():
+                late = yy == 0 and not CROSS_NEAR_FIRST[strand]
+                landed(pid[strand, "xnear" if late else "near"], near(strand))
+                if yy < 3:
+                    halo(strand, "far", near(strand), far(strand), y_dev[1])
+                else:
+                    halo(strand, "c2", near(strand), pst.at[strand, 1],
+                         next_dev if CROSS_FAR_FIRST[strand] else y_dev[1])
 
     def plus_done(strand):
-        landed(pid[strand, "far"], far(strand))
+        if CROSS_FAR_FIRST[strand]:
+            landed(pid[strand, "far"], far(strand))
+        else:
+            @pl.when(y == 0)
+            def _():
+                landed(pid[strand, "xfar"], far(strand))
+
+            @pl.when(y > 0)
+            def _():
+                landed(pid[strand, "far"], far(strand))
 
     def minus_start(strand):
-        m = strand - MINUS[0]
-        copy(pid[strand, "u1"], own(strand), sst.at[m, 0], y_dev[-1]).start()
+        halo(strand, "u1", own(strand), sst.at[strand - MINUS[0], 0], y_dev[-1])
 
     def minus_second(strand):
         m = strand - MINUS[0]
         landed(pid[strand, "u1"], sst.at[m, 0])
 
-        @pl.when(y == 3)
+        @pl.when((y == 0) | (y == 3))
         def _():
-            copy(pid[strand, "u2"], sst.at[m, 0], far(strand), y_dev[-1]).start()
-
-        @pl.when(y == 0)
-        def _():
-            copy(pid[strand, "u2"], sst.at[m, 0], far(strand), y_dev[-1]).start()
+            halo(strand, "u2", sst.at[m, 0], far(strand), y_dev[-1])
 
         @pl.when((y == 1) | (y == 2))
         def _():
-            copy(pid[strand, "u2"], sst.at[m, 0], sst.at[m, 1], y_dev[-1]).start()
+            halo(strand, "u2", sst.at[m, 0], sst.at[m, 1], y_dev[-1])
+
+    def minus_hand(strand):
+        m = strand - MINUS[0]
+
+        @pl.when(y <= 1)
+        def _():
+            landed(pid[strand, "u2"], sst.at[m, 1])
+            halo(strand, "cfar", sst.at[m, 1], far(strand), next_dev)
 
     def minus_third(strand):
         m = strand - MINUS[0]
@@ -178,64 +211,51 @@
         @pl.when(y >= 2)
         def _():
             landed(pid[strand, "u2"], far(strand))
-            copy(pid[strand, "u3"], far(strand), near(strand), y_dev[-1]).start()
-
+            halo(strand, "u3", far(strand), near(strand), y_dev[-1])
+
+        @pl.when(y == 0)
+        def _():
+            halo(strand, "u3", sst.at[m, 1], near(strand), y_dev[-1])
+
+    def minus_cross(strand):
         @pl.when(y == 1)
         def _():
-            landed(pid[strand, "u2"], sst.at[m, 1])
-            copy(pid[strand, "u3"], sst.at[m, 1], sst.at[m, 2], y_dev[-1]).start()
-            copy(pid[strand, "cfar"], sst.at[m, 1], far(strand), next_dev).start()
+            landed(pid[strand, "cfar"], far(strand))
+            halo(strand, "u3", far(strand), near(strand), y_dev[-1])
+
+    def minus_done(strand):
+        landed(pid[strand, "u3"], near(strand))
 
         @pl.when(y == 0)
         def _():
-            landed(pid[strand, "u2"], sst.at[m, 1])
-            copy(pid[strand, "u3"], sst.at[m, 1], near(strand), y_dev[-1]).start()
-            copy(pid[strand, "cfar"], sst.at[m, 1], far(strand), next_dev).start()
-
-    def minus_cross(strand):
-        m = strand - MINUS[0]
-
-        @pl.when(y == 0)
-        def _():
-            landed(pid[strand, "u3"], sst.at[m, 2])
-            copy(pid[strand, "cnear"], sst.at[m, 2], near(strand), next_dev).start()
-
-    def minus_done(strand):
-        @pl.when(y > 0)
-        def _():
-            landed(pid[strand, "u3"], near(strand))
-
-        @pl.when(y == 0)
-        def _():
-            landed(pid[strand, "cnear"], near(strand))
-
-        @pl.when(y <= 1)
-        def _():
             landed(pid[strand, "cfar"], far(strand))
 
     def halo_sends_done():
+        def done(condition, *which):
+            def wait():
+                for strand, name in which:
+                    copy(pid[strand, name], near(strand), near(strand), x_dev).wait_send()
+
+            if condition is None:
+                wait()
+            else:
+                pl.when(condition)(wait)
+
         for strand in PLUS:
-            piece = near(strand)
-            copy(pid[strand, "near"], piece, piece, x_dev).wait_send()
-            copy(pid[strand, "far"], piece, piece, x_dev).wait_send()
-
-            @pl.when(y == 3)
-            def _():
-                copy(pid[strand, "c3"], piece, piece, x_dev).wait_send()
-                copy(pid[strand, "c2"], piece, piece, x_dev).wait_send()
-
+            done(y == 3, (strand, "c3"), (strand, "c2"))
+            if CROSS_NEAR_FIRST[strand]:
+                done(None, (strand, "near"))
+            else:
+                done(y < 3, (strand, "near"))
+                done(y == 0, (strand, "xnear"))
+            if CROSS_FAR_FIRST[strand]:
+                done(None, (strand, "far"))
+            else:
+                done(y < 3, (strand, "far"))
+                done(y == 0, (strand, "xfar"))
         for strand in MINUS:
-            piece = near(strand)
-            for name in ("u1", "u2", "u3"):
-                copy(pid[strand, name], piece, piece, x_dev).wait_send()
-
-            @pl.when(y <= 1)
-            def _():
-                copy(pid[strand, "cfar"], piece, piece, x_dev).wait_send()
-
-            @pl.when(y == 0)
-            def _():
-                copy(pid[strand, "cnear"], piece, piece, x_dev).wait_send()
+            done(None, (strand, "u1"), (strand, "u2"), (strand, "u3"))
+            done(y <= 1, (strand, "cfar"))
 
     def gradients(h):
         hc = pl.ds(h * HD, HD)
@@ -366,7 +386,11 @@
     out_row = mult(32 * s_own + 16 * lax.rem(y, 2), 16)
 
     def renorm():
-        total = ys[y].astype(F32)
+        in_piece = pl.ds(mult(16 * y, 16), 16)
+        out_piece = pl.ds(mult(64 + 16 * lax.rem(y, 2), 16), 16)
+        total = jnp.concatenate(
+            [u0[in_piece], u1[in_piece], jnp.where(y < 2, u0[out_piece], u1[out_piece])], axis=0
+        )
         for j in range(3):
             total = total + yr[j].astype(F32)
         for h in (0, 1):
@@ -457,6 +481,9 @@
     col = lax.broadcasted_iota(jnp.int32, (256, 256), 1)
     far_off = jnp.where(c < 2, 1e30, 0.0).astype(F32)
     near_off = jnp.where(c < 1, 1e30, 0.0).astype(F32)
+
+    attended_heads = set()
+    applied_heads = set()
 
     def attention(a, rb):
         ac = pl.ds(a * ADIM, ADIM)
@@ -479,7 +506,12 @@
         total = sum(jnp.sum(w, axis=1, keepdims=True) for w in weights)
         probs = jnp.concatenate([w.astype(BF) for w in weights], axis=1)
         mixed = nn(probs, kv[1, window, ac])
-        att[pl.ds(rb * 256, 256), ac] = mixed / total
+        rows = pl.ds(rb * 256, 256)
+        if a // 5 in applied_heads:
+            out[rows, ac] = (att[rows, ac] + mixed / total).astype(BF)
+        else:
+            att[rows, ac] = mixed / total
+        attended_heads.add(a)
 
     def attend(strand):
         for a in (2 * strand, 2 * strand + 1):
@@ -497,37 +529,43 @@
         old_norm = jnp.sqrt(jnp.sum(old * old, axis=0, keepdims=True))
         new_norm = jnp.sqrt(jnp.sum(new * new, axis=0, keepdims=True))
         applied = nn(hidden, mo[h]) * (old_norm / (new_norm + EPS))
-        out[:, hc] = (att[:, hc] + applied).astype(BF)
+        for a in range(5 * h, 5 * h + 5):
+            ac = pl.ds(a * ADIM, ADIM)
+            part = applied[:, (a - 5 * h) * ADIM:(a - 5 * h + 1) * ADIM]
+            if a in attended_heads:
+                out[:, ac] = (att[:, ac] + part).astype(BF)
+            else:
+                att[:, ac] = part
+        applied_heads.add(h)
 
     plus_start(0)
     minus_start(3)
+    plus_start(1, rest=False)
     locals_[0].wait()
     locals_[1].wait()
     locals_[2].wait()
     gradients(0)
     cross0_start()
-    plus_start(1)
+    plus_start(1, last=False)
     minus_start(4)
     gradients(1)
     ring1_step(0)
-    plus_start(2)
     ring1_step(1)
-    plus_cross_near(0)
-    plus_forward(0)
+    plus_relay_near(0)
+    plus_relay_near(1)
+    plus_forward(0, (1, 2, 3))
+    minus_second(3)
     ring1_step(2)
-    minus_second(3)
     ring1_step(3)
+    plus_forward(0, (0,))
     ring0_step(0)
+    ring0_step(1)
     ring1_end()
-    plus_cross_near(1)
-    plus_forward(1)
-    minus_second(4)
-    ring0_step(1)
-    plus_cross_far(0)
-    plus_cross_near(2)
+    plus_start(2, rest=False)
+    plus_forward(1, (3,))
     ring0_step(2)
-    minus_third(3)
-    plus_forward(2)
+    minus_hand(3)
+    plus_relay_far(0)
     ring0_step(3)
     ring0_end()
     y_reduce()
@@ -536,36 +574,44 @@
     gather_send(0, 1)
     push(share1, chunk(1, z, None, x), x_dev)
     share_send(0)
-    plus_cross_far(1)
-    minus_third(4)
+    plus_start(2, last=False)
+    plus_relay_near(2)
+    minus_third(3)
+    minus_second(4)
+    plus_forward(1, (0, 1, 2))
+    minus_cross(3)
     pushed(share1, chunk(1, z, None, other))
     gather_send(1, 1)
     locals_[3].wait()
-    plus_done(0)
     for j in (1, 2, 3):
         gather_wait(0, j)
         gather_send(0, j + 1)
         share_send(j)
-        if j == 1:
-            plus_cross_far(2)
-            minus_cross(3)
-        if j == 2:
-            minus_cross(4)
         gather_wait(1, j)
         gather_send(1, j + 1)
+        if j == 1:
+            plus_relay_far(1)
+        if j == 2:
+            plus_done(0)
+            attend(0)
+            minus_hand(4)
+            minus_third(4)
+            plus_forward(2)
+        if j == 3:
+            minus_done(3)
+            attend(3)
     gather_wait(0, 4)
     share_send(4)
-    attend(0)
     plus_done(1)
     attend(1)
+    plus_relay_far(2)
+    minus_cross(4)
+    gather_wait(1, 4)
+    apply(1)
+    minus_done(4)
+    attend(4)
     plus_done(2)
     attend(2)
-    minus_done(3)
-    attend(3)
-    minus_done(4)
-    attend(4)
-    gather_wait(1, 4)
-    apply(1)
     share_wait()
     apply(0)
     halo_sends_done()
@@ -599,7 +645,7 @@
             pltpu.VMEM((4, 48, HD), BF),
             pltpu.VMEM((3, 48, HD), BF),
             pltpu.VMEM((3, 2, 2, TOK, STRAND), BF),
-            pltpu.VMEM((2, 3, 2, TOK, STRAND), BF),
+            pltpu.VMEM((2, 2, 2, TOK, STRAND), BF),
             pltpu.VMEM((TOK, COLS), F32),
             pltpu.SemaphoreType.DMA((4,)),
             pltpu.SemaphoreType.DMA((MESSAGES,)),

time: 213 us -> 155 us (0.73)
  Pallas kernels: 205 us -> 146 us
    pallas_call x1, Pallas kernels: 205 us -> 146 us  [local(): pl.pallas_call(kernel, out_shape=jax.ShapeDtypeStruct((TOK, COLS), BF), i...]
where the time goes in v2:
time: 155 us; the launch traced here: 154 us
  Pallas kernels  146 us (94%)
  local copies, waits for them, and re-layouts  8.38 us (5%)
    pallas_call x1, Pallas kernels, local(): pl.pallas_call(kernel, out_shape=jax.ShapeDtypeStruct((TOK, COLS), BF), i...  146 us
    unnamed x3, local copies, waits for them, and re-layouts  8.38 us

profile of v2, /device:TPU:2, one launch (start us, length us, event | category | flops | bytes accessed | tf_op | source)
XLA Modules:
  0.0 154.3 jit_solution(15427827264778411145)
XLA Ops:
  0.0 1.5 copy.6.step
  1.5 4.4 %copy.5 = bf16[2,640,1024]{1,2,0:T(8,128)(2,1)} copy(bf16[2,640,1024]{2,1,0:T(8,128)(2,1)} %param.6) | data formatting | bytes 5242880 | tf_op args[2]
  5.9 145.9 %ttt_layer.1 = bf16[512,1280]{1,0:T(8,128)(2,1)} custom-call(bf16[3,512,1280]{2,1,0:T(8,128)(2,1)} %qkv.1, f32[512,2]{1,0:T(8,128)} %copy.6.step, bf16[2,1024,640]{2,1,0:T(8,128)(2,1)} %bitcast.1, bf16[2,512,640]{2,1,0:T(8,128)(2,1)} %w_out.1), custom_call_target="tpu_custom_call" | custom-call | tf_op jit(solution)/shard_map/ttt_layer/pallas_call | solution.py:625
  151.8 2.5 %copy.8 = bf16[512,1280]{1,0:T(8,128)(2,1)} copy(bf16[512,1280]{1,0:T(8,128)(2,1)} %ttt_layer.1) | data formatting | bytes 2621440

commit v3 on v2

--- a/solution.py
+++ b/solution.py
@@ -20,6 +20,7 @@
 MINUS = (3, 4)
 CROSS_NEAR_FIRST = {0: True, 1: False, 2: True}
 CROSS_FAR_FIRST = {0: False, 1: True, 2: True}
+VIA = {(1, "c2"): 0, (0, "xfar"): 1, (3, "cfar"): 2}
 BF = jnp.bfloat16
 F32 = jnp.float32
 MESH = pl.DeviceIdType.MESH
@@ -40,7 +41,7 @@
 
 def kernel(
     qkv, step, w_in, w_out, out,
-    kv, q, wi, wo, g, mi, mo, r1, r0, xb, x1, t1, u0, u1, ys, yr, pst, sst, att,
+    kv, q, wi, wo, g, mi, mo, r1, r0, xb, x1, t1, u0, u1, ys, yr, pst, sst, vst, att,
     local_sem, ss, rs,
 ):
     c = lax.axis_index("ctx")
@@ -119,8 +120,48 @@
         for name in ("u1", "u2", "u3", "cfar"):
             pid[strand, name] = message(None, False)
 
+    for strand, name in VIA:
+        for leg in ("v", "r"):
+            pid[strand, name + leg] = message(None, False)
+
     def halo(strand, name, src, dst, device):
         copy(pid[strand, name], src, dst, device).start()
+
+    def cross(strand, name, src, dst):
+        if (strand, name) not in VIA:
+            halo(strand, name, src, dst, next_dev)
+            return
+
+        @pl.when(x == 0)
+        def _():
+            halo(strand, name, src, dst, next_dev)
+
+        @pl.when(x == 1)
+        def _():
+            halo(strand, name + "v", src, vst.at[VIA[strand, name]], x_dev)
+
+    def relay(strand, name, where, dst):
+        if (strand, name) not in VIA:
+            return
+
+        @pl.when((x == 0) & where)
+        def _():
+            stage = vst.at[VIA[strand, name]]
+            landed(pid[strand, name + "v"], stage)
+            halo(strand, name + "r", stage, dst, z_dev[0])
+
+    def crossed(strand, name, dst):
+        if (strand, name) not in VIA:
+            landed(pid[strand, name], dst)
+            return
+
+        @pl.when(x == 0)
+        def _():
+            landed(pid[strand, name + "r"], dst)
+
+        @pl.when(x == 1)
+        def _():
+            landed(pid[strand, name], dst)
 
     def plus_start(strand, last=True, rest=True):
         if rest:
@@ -150,13 +191,13 @@
         if CROSS_FAR_FIRST[strand]:
             @pl.when(y == 3)
             def _():
-                landed(pid[strand, "c2"], pst.at[strand, 1])
+                crossed(strand, "c2", pst.at[strand, 1])
                 halo(strand, "far", pst.at[strand, 1], far(strand), y_dev[1])
         else:
             @pl.when(y == 0)
             def _():
                 landed(pid[strand, "c2"], pst.at[strand, 1])
-                halo(strand, "xfar", pst.at[strand, 1], far(strand), next_dev)
+                cross(strand, "xfar", pst.at[strand, 1], far(strand))
 
     def plus_forward(strand, ys_=(0, 1, 2, 3)):
         for yy in ys_:
@@ -167,8 +208,10 @@
                 if yy < 3:
                     halo(strand, "far", near(strand), far(strand), y_dev[1])
                 else:
-                    halo(strand, "c2", near(strand), pst.at[strand, 1],
-                         next_dev if CROSS_FAR_FIRST[strand] else y_dev[1])
+                    if CROSS_FAR_FIRST[strand]:
+                        cross(strand, "c2", near(strand), pst.at[strand, 1])
+                    else:
+                        halo(strand, "c2", near(strand), pst.at[strand, 1], y_dev[1])
 
     def plus_done(strand):
         if CROSS_FAR_FIRST[strand]:
@@ -176,7 +219,7 @@
         else:
             @pl.when(y == 0)
             def _():
-                landed(pid[strand, "xfar"], far(strand))
+                crossed(strand, "xfar", far(strand))
 
             @pl.when(y > 0)
             def _():
@@ -203,7 +246,7 @@
         @pl.when(y <= 1)
         def _():
             landed(pid[strand, "u2"], sst.at[m, 1])
-            halo(strand, "cfar", sst.at[m, 1], far(strand), next_dev)
+            cross(strand, "cfar", sst.at[m, 1], far(strand))
 
     def minus_third(strand):
         m = strand - MINUS[0]
@@ -220,7 +263,7 @@
     def minus_cross(strand):
         @pl.when(y == 1)
         def _():
-            landed(pid[strand, "cfar"], far(strand))
+            crossed(strand, "cfar", far(strand))
             halo(strand, "u3", far(strand), near(strand), y_dev[-1])
 
     def minus_done(strand):
@@ -228,18 +271,22 @@
 
         @pl.when(y == 0)
         def _():
-            landed(pid[strand, "cfar"], far(strand))
+            crossed(strand, "cfar", far(strand))
 
     def halo_sends_done():
+        def wait(condition, strand, name):
+            @pl.when(condition)
+            def _():
+                copy(pid[strand, name], near(strand), near(strand), x_dev).wait_send()
+
         def done(condition, *which):
-            def wait():
-                for strand, name in which:
-                    copy(pid[strand, name], near(strand), near(strand), x_dev).wait_send()
-
-            if condition is None:
-                wait()
-            else:
-                pl.when(condition)(wait)
+            for strand, name in which:
+                if (strand, name) in VIA:
+                    wait(condition & (x == 0), strand, name)
+                    wait(condition & (x == 1), strand, name + "v")
+                    wait(condition & (x == 0), strand, name + "r")
+                else:
+                    wait(y >= 0 if condition is None else condition, strand, name)
 
         for strand in PLUS:
             done(y == 3, (strand, "c3"), (strand, "c2"))
@@ -261,7 +308,7 @@
         hc = pl.ds(h * HD, HD)
         keys = kv[0, own_rows, hc]
         vals = kv[1, own_rows, hc]
-        rate = step[:, h:h + 1]
+        rate = jnp.broadcast_to(step[h:h + 1, :], (8, TOK)).T[:, 0:1]
         scaled = (rate * vals.astype(F32)).astype(BF)
         gate = nt(wi[h, 0:FH], keys)
         up = nt(wi[h, FH:2 * FH], keys)
@@ -579,7 +626,8 @@
     minus_third(3)
     minus_second(4)
     plus_forward(1, (0, 1, 2))
-    minus_cross(3)
+    relay(1, "c2", y == 3, pst.at[1, 1])
+    relay(3, "cfar", y <= 1, far(3))
     pushed(share1, chunk(1, z, None, other))
     gather_send(1, 1)
     locals_[3].wait()
@@ -590,7 +638,10 @@
         gather_wait(1, j)
         gather_send(1, j + 1)
         if j == 1:
+            relay(0, "xfar", y == 0, far(0))
+        if j == 2:
             plus_relay_far(1)
+            minus_cross(3)
         if j == 2:
             plus_done(0)
             attend(0)
@@ -646,6 +697,7 @@
             pltpu.VMEM((3, 48, HD), BF),
             pltpu.VMEM((3, 2, 2, TOK, STRAND), BF),
             pltpu.VMEM((2, 2, 2, TOK, STRAND), BF),
+            pltpu.VMEM((len(VIA), 2, TOK, STRAND), BF),
             pltpu.VMEM((TOK, COLS), F32),
             pltpu.SemaphoreType.DMA((4,)),
             pltpu.SemaphoreType.DMA((MESSAGES,)),
@@ -655,7 +707,7 @@
         compiler_params=pltpu.CompilerParams(
             collective_id=0, has_side_effects=True, vmem_limit_bytes=62 * 2**20
         ),
-    )(qkv, step_size, fast_in.transpose(0, 2, 1), fast_out)
+    )(qkv, step_size.T, fast_in.transpose(0, 2, 1), fast_out)
 
 
 def solution(mesh):

time: 155 us -> 140 us (0.903)
  Pallas kernels: 146 us -> 132 us
    pallas_call x1, Pallas kernels: 146 us -> 132 us  [local(): pl.pallas_call(kernel, out_shape=jax.ShapeDtypeStruct((TOK, COLS), BF), i...]
    unnamed x3 -> x2, local copies, waits for them, and re-layouts: 8.38 us -> 6.84 us
where the time goes in v3:
time: 140 us; the launch traced here: 139 us
  Pallas kernels  132 us (94%)
  local copies, waits for them, and re-layouts  6.84 us (5%)
    pallas_call x1, Pallas kernels, local(): pl.pallas_call(kernel, out_shape=jax.ShapeDtypeStruct((TOK, COLS), BF), i...  132 us
    unnamed x2, local copies, waits for them, and re-layouts  6.84 us

profile of v3, /device:TPU:2, one launch (start us, length us, event | category | flops | bytes accessed | tf_op | source)
XLA Modules:
  0.0 138.6 jit_solution(6640366664211558695)
XLA Ops:
  0.0 4.4 %copy.5 = bf16[2,640,1024]{1,2,0:T(8,128)(2,1)} copy(bf16[2,640,1024]{2,1,0:T(8,128)(2,1)} %param.6) | data formatting | bytes 5242880 | tf_op args[2]
  4.4 131.8 %ttt_layer.1 = bf16[512,1280]{1,0:T(8,128)(2,1)} custom-call(bf16[3,512,1280]{2,1,0:T(8,128)(2,1)} %qkv.1, f32[2,512]{1,0:T(2,128)} %bitcast.3, bf16[2,1024,640]{2,1,0:T(8,128)(2,1)} %bitcast.2, bf16[2,512,640]{2,1,0:T(8,128)(2,1)} %w_out.1), custom_call_target="tpu_custom_call" | custom-call | tf_op jit(solution)/shard_map/ttt_layer/pallas_call | solution.py:676
  136.2 2.5 %copy.7 = bf16[512,1280]{1,0:T(8,128)(2,1)} copy(bf16[512,1280]{1,0:T(8,128)(2,1)} %ttt_layer.1) | data formatting | bytes 2621440

commit v4 on v3

--- a/solution.py
+++ b/solution.py
@@ -41,7 +41,7 @@
 
 def kernel(
     qkv, step, w_in, w_out, out,
-    kv, q, wi, wo, g, mi, mo, r1, r0, xb, x1, t1, u0, u1, ys, yr, pst, sst, vst, att,
+    kv, q, raw, wi, wo, g, mi, mo, r1, r0, xb, x1, t1, u0, u1, ys, yr, pst, sst, vst, att,
     local_sem, ss, rs,
 ):
     c = lax.axis_index("ctx")
@@ -94,8 +94,8 @@
     own_rows = pl.ds(2 * TOK, TOK)
     near_rows = pl.ds(TOK, TOK)
     far_rows = pl.ds(0, TOK)
+    fetch(w_in, raw)
     fetch(qkv.at[pl.ds(1, 2)], kv.at[:, own_rows])
-    fetch(w_in, wi)
     fetch(w_out, wo)
     fetch(qkv.at[0], q)
     pl.semaphore_wait(barrier, 8)
@@ -310,6 +310,8 @@
         vals = kv[1, own_rows, hc]
         rate = jnp.broadcast_to(step[h:h + 1, :], (8, TOK)).T[:, 0:1]
         scaled = (rate * vals.astype(F32)).astype(BF)
+        for part in range(4):
+            wi[h, 256 * part:256 * part + 256] = raw[h, :, 256 * part:256 * part + 256].T
         gate = nt(wi[h, 0:FH], keys)
         up = nt(wi[h, FH:2 * FH], keys)
         back = nt(wo[h], scaled)
@@ -605,6 +607,8 @@
     ring1_step(2)
     ring1_step(3)
     plus_forward(0, (0,))
+    minus_second(4)
+    plus_start(2, last=False)
     ring0_step(0)
     ring0_step(1)
     ring1_end()
@@ -621,10 +625,8 @@
     gather_send(0, 1)
     push(share1, chunk(1, z, None, x), x_dev)
     share_send(0)
-    plus_start(2, last=False)
     plus_relay_near(2)
     minus_third(3)
-    minus_second(4)
     plus_forward(1, (0, 1, 2))
     relay(1, "c2", y == 3, pst.at[1, 1])
     relay(3, "cfar", y <= 1, far(3))
@@ -661,10 +663,10 @@
     apply(1)
     minus_done(4)
     attend(4)
+    share_wait()
+    apply(0)
     plus_done(2)
     attend(2)
-    share_wait()
-    apply(0)
     halo_sends_done()
     for index, ref in sent:
         copy(index, ref, ref, x_dev).wait_send()
@@ -681,6 +683,7 @@
         scratch_shapes=[
             pltpu.VMEM((2, 3 * TOK, COLS), BF),
             pltpu.VMEM((TOK, COLS), BF),
+            pltpu.VMEM((2, HD, 2 * FH), BF),
             pltpu.VMEM((2, 2 * FH, HD), BF),
             pltpu.VMEM((2, FH, HD), BF),
             pltpu.VMEM((2, 16, 96, HD), BF),
@@ -707,7 +710,7 @@
         compiler_params=pltpu.CompilerParams(
             collective_id=0, has_side_effects=True, vmem_limit_bytes=62 * 2**20
         ),
-    )(qkv, step_size.T, fast_in.transpose(0, 2, 1), fast_out)
+    )(qkv, step_size.T, fast_in, fast_out)
 
 
 def solution(mesh):

time: 140 us -> 136 us (0.971)
  local copies, waits for them, and re-layouts: 6.84 us -> 2.46 us
    unnamed x2 -> x1, local copies, waits for them, and re-layouts: 6.84 us -> 2.46 us
where the time goes in v4:
time: 136 us; the launch traced here: 135 us
  Pallas kernels  133 us (98%)
  local copies, waits for them, and re-layouts  2.46 us (2%)
    pallas_call x1, Pallas kernels, local(): pl.pallas_call(kernel, out_shape=jax.ShapeDtypeStruct((TOK, COLS), BF), i...  133 us

profile of v4, /device:TPU:2, one launch (start us, length us, event | category | flops | bytes accessed | tf_op | source)
XLA Modules:
  0.0 135.3 jit_solution(7533397648355704423)
XLA Ops:
  0.0 132.8 %ttt_layer.1 = bf16[512,1280]{1,0:T(8,128)(2,1)} custom-call(bf16[3,512,1280]{2,1,0:T(8,128)(2,1)} %qkv.1, f32[2,512]{1,0:T(2,128)} %bitcast.1, bf16[2,640,1024]{2,1,0:T(8,128)(2,1)} %w_in.1, bf16[2,512,640]{2,1,0:T(8,128)(2,1)} %w_out.1), custom_call_target="tpu_custom_call" | custom-call | tf_op jit(solution)/shard_map/ttt_layer/pallas_call | solution.py:678
  132.9 2.5 %copy.6 = bf16[512,1280]{1,0:T(8,128)(2,1)} copy(bf16[512,1280]{1,0:T(8,128)(2,1)} %ttt_layer.1) | data formatting | bytes 2621440

commit v5 on v4

--- a/solution.py
+++ b/solution.py
@@ -499,21 +499,19 @@
             landed(index, ref)
 
     gather = {
-        (h, j, d): pair_ids(h, d if j == 4 else None)
-        for h in (0, 1) for j in (1, 2, 3, 4) for d in (0, 1)
+        (h, j, d): pair_ids(h)
+        for h in (0, 1) for j in (1, 2, 3, 4) for d in (0, 1) if (j, d) != (4, 0)
     }
     share0 = [pair_ids(0) for _ in range(8)]
     share1 = pair_ids(1, None, x)
 
     def gather_send(h, j):
-        for d in (0, 1):
-            part = d if j == 4 else None
-            push(gather[h, j, d], chunk(h, z_of(1 - d, j - 1), part), z_dev[d])
+        for d in (0, 1) if j < 4 else (1,):
+            push(gather[h, j, d], chunk(h, z_of(1 - d, j - 1)), z_dev[d])
 
     def gather_wait(h, j):
-        for d in (0, 1):
-            part = d if j == 4 else None
-            pushed(gather[h, j, d], chunk(h, z_of(1 - d, j), part))
+        for d in (0, 1) if j < 4 else (1,):
+            pushed(gather[h, j, d], chunk(h, z_of(1 - d, j)))
 
     share_order = [(0, 0)] + [(d, j) for j in (1, 2, 3) for d in (0, 1)] + [(0, 4)]
 

time: 136 us -> 135 us (level)
  no operation moved by 1% of the time
where the time goes in v5:
time: 135 us
  Pallas kernels  132 us (98%)
  local copies, waits for them, and re-layouts  2.46 us (2%)
    pallas_call x1, Pallas kernels, local(): pl.pallas_call(kernel, out_shape=jax.ShapeDtypeStruct((TOK, COLS), BF), i...  132 us

profile of v5, /device:TPU:2, one launch (start us, length us, event | category | flops | bytes accessed | tf_op | source)
XLA Modules:
  0.0 134.7 jit_solution(7285054794161583600)
XLA Ops:
  0.0 132.2 %ttt_layer.1 = bf16[512,1280]{1,0:T(8,128)(2,1)} custom-call(bf16[3,512,1280]{2,1,0:T(8,128)(2,1)} %qkv.1, f32[2,512]{1,0:T(2,128)} %bitcast.1, bf16[2,640,1024]{2,1,0:T(8,128)(2,1)} %w_in.1, bf16[2,512,640]{2,1,0:T(8,128)(2,1)} %w_out.1), custom_call_target="tpu_custom_call" | custom-call | tf_op jit(solution)/shard_map/ttt_layer/pallas_call | solution.py:676
  132.2 2.5 %copy.6 = bf16[512,1280]{1,0:T(8,128)(2,1)} copy(bf16[512,1280]{1,0:T(8,128)(2,1)} %ttt_layer.1) | data formatting | bytes 2621440
